TPU v7x, 32 devices: a whole 2x2x4 slice. The times are simulated.
32 devices in a mesh: obs: 2 (over x), chan: 16 (over z, y, core).
Axes of the slice: x: 2, y: 2, z: 4, core: 2. Of those that a mesh axis runs over, the one named last changes fastest.
Arguments:
- voltages: bfloat16 [2, 1024, 512, 256], P(None, ('obs', 'chan')), parts along dimension 1, may hold values from -6 to 6
- cal_gains: int32 [2, 1024, 512], P(None, ('obs', 'chan')), parts along dimension 1, may hold values from -65536 to 65536
- beam_phase: int32 [512, 512], replicated, may hold values from 0 to 1023
- delays: int32 [128, 512], replicated, may hold values from 0 to 255
Outputs:
- dedispersed: float32 [1024, 128, 256], P(('obs', 'chan')), parts along dimension 0
There are 2 independent parts, one for each index of `obs`. A program takes and returns all parts, laid end to end along the dimension named above; an argument that names none is the same for every part. Nothing has to cross between parts.
All inputs are finite; a program needn't handle non-finite values.
Results may differ from a plain program's by a relative error of at most 0.0071.
Values may be sent and summed in bfloat16 or wider, within the bound.
A program may use at most 192 MiB of HBM per device.

v0:
```python
import math

import jax
import jax.numpy as jnp
from jax import lax
from jax.sharding import PartitionSpec as P

PHASES = 1024


def beam_matrix(beam_phase):
    station_count = beam_phase.shape[1]
    angles = beam_phase.astype(jnp.float32) * (2.0 * math.pi / PHASES)
    scaling = 1.0 / math.sqrt(station_count)
    real_part = jnp.cos(angles) * scaling
    imag_part = jnp.sin(angles) * scaling
    upper_rows = jnp.concatenate([real_part, -imag_part], axis=1)
    bottom = jnp.concatenate([imag_part, real_part], axis=1)
    return jnp.concatenate([upper_rows, bottom], axis=0).astype(jnp.bfloat16)


def detect(weights, received):
    station_count = received.shape[1]
    item_count = received.shape[3]
    time_count = received.shape[4]
    flattened = received.reshape(2 * station_count, item_count * time_count)
    beam_sum = jnp.dot(weights, flattened, preferred_element_type=jnp.float32)
    beam_count = weights.shape[0] // 2
    powers = beam_sum[:beam_count] ** 2 + beam_sum[beam_count:] ** 2
    return powers.reshape(beam_count, item_count, time_count).astype(jnp.bfloat16)


def dedisperse(arrived, delays):
    chans = arrived.shape[1]
    time_count = arrived.shape[2]
    precise = lax.Precision.HIGH
    series = arrived.astype(jnp.float32)
    centred = series - jnp.mean(series, axis=2, keepdims=True)
    fblock = min(16, time_count)
    half_count = time_count // 2 + 1
    nblocks = (half_count + fblock - 1) // fblock
    freq_count = nblocks * fblock
    sample_index = jnp.arange(time_count, dtype=jnp.int32)
    freq_index = jnp.arange(freq_count, dtype=jnp.int32)
    product_grid = sample_index[:, None] * freq_index[None, :] % time_count
    grid_angles = product_grid.astype(jnp.float32) * (2.0 * math.pi / time_count)
    cos_table = jnp.cos(grid_angles)
    sin_table = jnp.sin(grid_angles)
    inner = (freq_index > 0) & (freq_index < time_count // 2)
    edges = (freq_index == 0) | (freq_index == time_count // 2)
    freq_weight = jnp.where(inner, 2.0, jnp.where(edges, 1.0, 0.0)).astype(jnp.float32)
    spec_real = jnp.einsum("bct,tf->fbc", centred, cos_table, precision=precise)
    spec_imag = -jnp.einsum("bct,tf->fbc", centred, sin_table, precision=precise)

    def spectrum(offset):
        frequency = offset + jnp.arange(fblock, dtype=jnp.int32)
        phase_level = frequency[:, None, None] * delays[None, :, :] % time_count
        rotation = phase_level.astype(jnp.float32) * (2.0 * math.pi / time_count)
        cos_rot = jnp.cos(rotation)
        sin_rot = jnp.sin(rotation)
        part_real = lax.dynamic_slice_in_dim(spec_real, offset, fblock, 0)
        part_imag = lax.dynamic_slice_in_dim(spec_imag, offset, fblock, 0)
        out_real = jnp.einsum("fbc,fdc->fbd", part_real, cos_rot, precision=precise) - jnp.einsum(
            "fbc,fdc->fbd", part_imag, sin_rot, precision=precise
        )
        out_imag = jnp.einsum("fbc,fdc->fbd", part_real, sin_rot, precision=precise) + jnp.einsum(
            "fbc,fdc->fbd", part_imag, cos_rot, precision=precise
        )
        return (out_real, out_imag)

    offsets = jnp.arange(nblocks, dtype=jnp.int32) * fblock
    out_real, out_imag = lax.map(spectrum, offsets)
    out_real = out_real.reshape(freq_count, out_real.shape[2], out_real.shape[3])
    out_imag = out_imag.reshape(freq_count, out_imag.shape[2], out_imag.shape[3])
    back_cos = cos_table * freq_weight[None, :]
    back_sin = sin_table * freq_weight[None, :]
    result = jnp.einsum("fbd,tf->bdt", out_real, back_cos, precision=precise) - jnp.einsum(
        "fbd,tf->bdt", out_imag, back_sin, precision=precise
    )
    return result / (time_count * math.sqrt(chans))


def body(voltages, cal_gains, beam_phase, delays):
    gains = cal_gains.astype(jnp.float32) / 65536.0
    gain_real = gains[0][:, :, None]
    gain_imag = gains[1][:, :, None]
    volt_real = voltages[0].astype(jnp.float32)
    volt_imag = voltages[1].astype(jnp.float32)
    calibrated = jnp.stack(
        [
            volt_real * gain_real - volt_imag * gain_imag,
            volt_real * gain_imag + volt_imag * gain_real,
        ]
    ).astype(jnp.bfloat16)
    weights = beam_matrix(beam_phase)
    group_count = lax.axis_size("chan")
    station_local = calibrated.shape[1]
    channel_count = calibrated.shape[2]
    time_count = calibrated.shape[3]
    regrouped_in = calibrated.reshape(
        2, station_local, group_count, channel_count // group_count, time_count
    )
    received = lax.all_to_all(regrouped_in, "chan", split_axis=2, concat_axis=1, tiled=True)
    powers = detect(weights, received)
    arrived = lax.all_to_all(powers, "chan", split_axis=0, concat_axis=1, tiled=True)
    return dedisperse(arrived, delays)


def solution(mesh):
    return jax.shard_map(
        body,
        mesh=mesh,
        in_specs=(P(None, ("obs", "chan"), None, None), P(None, ("obs", "chan"), None), P(), P()),
        out_specs=P(("obs", "chan"), None, None),
        check_vma=False,
    )
```

profile of v0, /device:TPU:13, one launch (start us, length us, event | category | flops | bytes accessed | tf_op | source)
XLA Modules:
  0.0 1438.7 jit_solution(6616143904223047618)
XLA Ops:
  30.4 358.2 %all-to-all-done = bf16[2,32,16,32,256]{4,3,1,0,2:T(8,128)(2,1)} async-done(((bf16[2,32,16,32,256]{4,3,1,0,2:T(8,128)(2,1)}), bf16[2,32,16,32,256]{4,3,1,0,2:T(8,128)(2,1)}, u32[]{:S(2)}, u32[]{:S(2)}) %all-to-all-start) | async-done | bytes 16777248 | tf_op jit(solution)/shard_map/all_to_all | solution.py:103
  410.6 26.8 %fusion.63 = f32[1024,8192]{1,0:T(8,128)} fusion(bf16[1024,8192]{1,0:T(8,128)(2,1)} %bitcast.61, bf16[512,512]{1,0:T(8,128)(2,1)S(1)} %get-tuple-element.160, bf16[512,512]{1,0:T(8,128)(2,1)S(1)} %get-tuple-element.159, bf16[512,512]{1,0:T(8,128)(2,1)S(1)} %get-tuple-element.158), kind=kOutput, calls=%fused_computation.64 | convolution fusion | flops 17188257792 | bytes 51904512 | tf_op jit(solution)/shard_map/dot_general | solution.py:27
  466.8 182.3 %all-to-all-done.1 = bf16[512,32,256]{2,1,0:T(8,128)(2,1)} async-done(((bf16[512,32,256]{2,1,0:T(8,128)(2,1)}), bf16[512,32,256]{2,1,0:T(8,128)(2,1)}, u32[]{:S(2)}, u32[]{:S(2)}) %all-to-all-start.1) | async-done | bytes 8388640 | tf_op jit(solution)/shard_map/all_to_all | solution.py:105
  690.3 18.5 %convolution_negate_fusion = f32[144,32,512]{2,0,1:T(8,128)} fusion(f32[32,512,256]{2,1,0:T(8,128)} %bitcast_subtract_fusion), kind=kOutput, calls=%fused_computation.59 | convolution fusion | flops 3626754048 | bytes 26214400 | tf_op jit(solution)/shard_map/bct,tf->fbc/dot_general | solution.py:53
  708.8 18.6 %fusion.78 = f32[144,32,512]{2,0,1:T(8,128)} fusion(f32[32,512,256]{2,1,0:T(8,128)} %bitcast_subtract_fusion), kind=kOutput, calls=%fused_computation.86 | convolution fusion | flops 3624394752 | bytes 26214400 | tf_op jit(solution)/shard_map/bct,tf->fbc/dot_general | solution.py:52
  727.5 697.8 %while.14 = (s32[]{:T(128)}, f32[9,16,32,128]{3,2,1,0:T(8,128)}, f32[9,16,32,128]{3,2,1,0:T(8,128)S(1)}, s32[9]{0:T(128)S(1)}, f32[144,32,512]{2,0,1:T(8,128)}, ...) while((s32[]{:T(128)}, f32[9,16,32,128]{3,2,1,0:T(8,128)}, ...), condition=%wide.region_2.3_spmd, body=%wide.region_1.2_spmd.sunk | while | flops 864157696 | bytes 11011487 | solution.py:72
  750.7 17.7 %fusion.140 = f32[9,16,32,128]{3,2,1,0:T(8,128)S(1)} fusion(f32[9,16,32,128]{3,2,1,0:T(8,128)S(1)} %get-tuple-element.222, s32[]{:T(128)} %get-tuple-element.220, f32[16,32,128]{2,1,0:T(8,128)S(1)} %fusion.139, s32[128,512]{1,0:T(8,128)S(1)} %get-tuple-element.235, s32[16]{0:T(128)S(1)} %iota_add_fusion.2, f32[16,32,512]{2,0,1:T(8,128)S(1)} %get-tuple-element.208), kind=kOutput, calls=%fused_computation.19.clone.1 | convolution fusion | flops 216072192 | bytes 1835524 | tf_op jit(solution)/shard_map/while/body/eval_jaxpr/fbc,fdc->fbd/dot_general | solution.py:66
  785.8 18.6 %fusion.138 = f32[9,16,32,128]{3,2,1,0:T(8,128)} fusion(f32[9,16,32,128]{3,2,1,0:T(8,128)} %get-tuple-element.221, s32[]{:T(128)} %get-tuple-element.220, f32[16,32,128]{2,1,0:T(8,128)S(1)} %fusion.137, s32[128,512]{1,0:T(8,128)S(1)} %get-tuple-element.235, s32[16]{0:T(128)S(1)} %iota_add_fusion.2, f32[16,32,512]{2,0,1:T(8,128)S(1)} %get-tuple-element.209), kind=kOutput, calls=%fused_computation.16.clone.1 | convolution fusion | flops 216072192 | bytes 1835584 | tf_op jit(solution)/shard_map/while/body/eval_jaxpr/fbc,fdc->fbd/dot_general | solution.py:63
  827.4 17.8 %fusion.140 = f32[9,16,32,128]{3,2,1,0:T(8,128)S(1)} fusion(f32[9,16,32,128]{3,2,1,0:T(8,128)S(1)} %get-tuple-element.222, s32[]{:T(128)} %get-tuple-element.220, f32[16,32,128]{2,1,0:T(8,128)S(1)} %fusion.139, s32[128,512]{1,0:T(8,128)S(1)} %get-tuple-element.235, s32[16]{0:T(128)S(1)} %iota_add_fusion.2, f32[16,32,512]{2,0,1:T(8,128)S(1)} %get-tuple-element.208), kind=kOutput, calls=%fused_computation.19.clone.1 | convolution fusion | flops 216072192 | bytes 1835524 | tf_op jit(solution)/shard_map/while/body/eval_jaxpr/fbc,fdc->fbd/dot_general | solution.py:66
  862.5 18.6 %fusion.138 = f32[9,16,32,128]{3,2,1,0:T(8,128)} fusion(f32[9,16,32,128]{3,2,1,0:T(8,128)} %get-tuple-element.221, s32[]{:T(128)} %get-tuple-element.220, f32[16,32,128]{2,1,0:T(8,128)S(1)} %fusion.137, s32[128,512]{1,0:T(8,128)S(1)} %get-tuple-element.235, s32[16]{0:T(128)S(1)} %iota_add_fusion.2, f32[16,32,512]{2,0,1:T(8,128)S(1)} %get-tuple-element.209), kind=kOutput, calls=%fused_computation.16.clone.1 | convolution fusion | flops 216072192 | bytes 1835584 | tf_op jit(solution)/shard_map/while/body/eval_jaxpr/fbc,fdc->fbd/dot_general | solution.py:63
  904.1 17.8 %fusion.140 = f32[9,16,32,128]{3,2,1,0:T(8,128)S(1)} fusion(f32[9,16,32,128]{3,2,1,0:T(8,128)S(1)} %get-tuple-element.222, s32[]{:T(128)} %get-tuple-element.220, f32[16,32,128]{2,1,0:T(8,128)S(1)} %fusion.139, s32[128,512]{1,0:T(8,128)S(1)} %get-tuple-element.235, s32[16]{0:T(128)S(1)} %iota_add_fusion.2, f32[16,32,512]{2,0,1:T(8,128)S(1)} %get-tuple-element.208), kind=kOutput, calls=%fused_computation.19.clone.1 | convolution fusion | flops 216072192 | bytes 1835524 | tf_op jit(solution)/shard_map/while/body/eval_jaxpr/fbc,fdc->fbd/dot_general | solution.py:66
  939.3 18.6 %fusion.138 = f32[9,16,32,128]{3,2,1,0:T(8,128)} fusion(f32[9,16,32,128]{3,2,1,0:T(8,128)} %get-tuple-element.221, s32[]{:T(128)} %get-tuple-element.220, f32[16,32,128]{2,1,0:T(8,128)S(1)} %fusion.137, s32[128,512]{1,0:T(8,128)S(1)} %get-tuple-element.235, s32[16]{0:T(128)S(1)} %iota_add_fusion.2, f32[16,32,512]{2,0,1:T(8,128)S(1)} %get-tuple-element.209), kind=kOutput, calls=%fused_computation.16.clone.1 | convolution fusion | flops 216072192 | bytes 1835584 | tf_op jit(solution)/shard_map/while/body/eval_jaxpr/fbc,fdc->fbd/dot_general | solution.py:63
  980.9 17.8 %fusion.140 = f32[9,16,32,128]{3,2,1,0:T(8,128)S(1)} fusion(f32[9,16,32,128]{3,2,1,0:T(8,128)S(1)} %get-tuple-element.222, s32[]{:T(128)} %get-tuple-element.220, f32[16,32,128]{2,1,0:T(8,128)S(1)} %fusion.139, s32[128,512]{1,0:T(8,128)S(1)} %get-tuple-element.235, s32[16]{0:T(128)S(1)} %iota_add_fusion.2, f32[16,32,512]{2,0,1:T(8,128)S(1)} %get-tuple-element.208), kind=kOutput, calls=%fused_computation.19.clone.1 | convolution fusion | flops 216072192 | bytes 1835524 | tf_op jit(solution)/shard_map/while/body/eval_jaxpr/fbc,fdc->fbd/dot_general | solution.py:66
  1016.1 18.6 %fusion.138 = f32[9,16,32,128]{3,2,1,0:T(8,128)} fusion(f32[9,16,32,128]{3,2,1,0:T(8,128)} %get-tuple-element.221, s32[]{:T(128)} %get-tuple-element.220, f32[16,32,128]{2,1,0:T(8,128)S(1)} %fusion.137, s32[128,512]{1,0:T(8,128)S(1)} %get-tuple-element.235, s32[16]{0:T(128)S(1)} %iota_add_fusion.2, f32[16,32,512]{2,0,1:T(8,128)S(1)} %get-tuple-element.209), kind=kOutput, calls=%fused_computation.16.clone.1 | convolution fusion | flops 216072192 | bytes 1835584 | tf_op jit(solution)/shard_map/while/body/eval_jaxpr/fbc,fdc->fbd/dot_general | solution.py:63
  1057.7 17.8 %fusion.140 = f32[9,16,32,128]{3,2,1,0:T(8,128)S(1)} fusion(f32[9,16,32,128]{3,2,1,0:T(8,128)S(1)} %get-tuple-element.222, s32[]{:T(128)} %get-tuple-element.220, f32[16,32,128]{2,1,0:T(8,128)S(1)} %fusion.139, s32[128,512]{1,0:T(8,128)S(1)} %get-tuple-element.235, s32[16]{0:T(128)S(1)} %iota_add_fusion.2, f32[16,32,512]{2,0,1:T(8,128)S(1)} %get-tuple-element.208), kind=kOutput, calls=%fused_computation.19.clone.1 | convolution fusion | flops 216072192 | bytes 1835524 | tf_op jit(solution)/shard_map/while/body/eval_jaxpr/fbc,fdc->fbd/dot_general | solution.py:66
  1092.8 18.6 %fusion.138 = f32[9,16,32,128]{3,2,1,0:T(8,128)} fusion(f32[9,16,32,128]{3,2,1,0:T(8,128)} %get-tuple-element.221, s32[]{:T(128)} %get-tuple-element.220, f32[16,32,128]{2,1,0:T(8,128)S(1)} %fusion.137, s32[128,512]{1,0:T(8,128)S(1)} %get-tuple-element.235, s32[16]{0:T(128)S(1)} %iota_add_fusion.2, f32[16,32,512]{2,0,1:T(8,128)S(1)} %get-tuple-element.209), kind=kOutput, calls=%fused_computation.16.clone.1 | convolution fusion | flops 216072192 | bytes 1835584 | tf_op jit(solution)/shard_map/while/body/eval_jaxpr/fbc,fdc->fbd/dot_general | solution.py:63
  1134.5 17.8 %fusion.140 = f32[9,16,32,128]{3,2,1,0:T(8,128)S(1)} fusion(f32[9,16,32,128]{3,2,1,0:T(8,128)S(1)} %get-tuple-element.222, s32[]{:T(128)} %get-tuple-element.220, f32[16,32,128]{2,1,0:T(8,128)S(1)} %fusion.139, s32[128,512]{1,0:T(8,128)S(1)} %get-tuple-element.235, s32[16]{0:T(128)S(1)} %iota_add_fusion.2, f32[16,32,512]{2,0,1:T(8,128)S(1)} %get-tuple-element.208), kind=kOutput, calls=%fused_computation.19.clone.1 | convolution fusion | flops 216072192 | bytes 1835524 | tf_op jit(solution)/shard_map/while/body/eval_jaxpr/fbc,fdc->fbd/dot_general | solution.py:66
  1169.6 18.6 %fusion.138 = f32[9,16,32,128]{3,2,1,0:T(8,128)} fusion(f32[9,16,32,128]{3,2,1,0:T(8,128)} %get-tuple-element.221, s32[]{:T(128)} %get-tuple-element.220, f32[16,32,128]{2,1,0:T(8,128)S(1)} %fusion.137, s32[128,512]{1,0:T(8,128)S(1)} %get-tuple-element.235, s32[16]{0:T(128)S(1)} %iota_add_fusion.2, f32[16,32,512]{2,0,1:T(8,128)S(1)} %get-tuple-element.209), kind=kOutput, calls=%fused_computation.16.clone.1 | convolution fusion | flops 216072192 | bytes 1835584 | tf_op jit(solution)/shard_map/while/body/eval_jaxpr/fbc,fdc->fbd/dot_general | solution.py:63
  1211.2 17.8 %fusion.140 = f32[9,16,32,128]{3,2,1,0:T(8,128)S(1)} fusion(f32[9,16,32,128]{3,2,1,0:T(8,128)S(1)} %get-tuple-element.222, s32[]{:T(128)} %get-tuple-element.220, f32[16,32,128]{2,1,0:T(8,128)S(1)} %fusion.139, s32[128,512]{1,0:T(8,128)S(1)} %get-tuple-element.235, s32[16]{0:T(128)S(1)} %iota_add_fusion.2, f32[16,32,512]{2,0,1:T(8,128)S(1)} %get-tuple-element.208), kind=kOutput, calls=%fused_computation.19.clone.1 | convolution fusion | flops 216072192 | bytes 1835524 | tf_op jit(solution)/shard_map/while/body/eval_jaxpr/fbc,fdc->fbd/dot_general | solution.py:66
  1246.4 18.6 %fusion.138 = f32[9,16,32,128]{3,2,1,0:T(8,128)} fusion(f32[9,16,32,128]{3,2,1,0:T(8,128)} %get-tuple-element.221, s32[]{:T(128)} %get-tuple-element.220, f32[16,32,128]{2,1,0:T(8,128)S(1)} %fusion.137, s32[128,512]{1,0:T(8,128)S(1)} %get-tuple-element.235, s32[16]{0:T(128)S(1)} %iota_add_fusion.2, f32[16,32,512]{2,0,1:T(8,128)S(1)} %get-tuple-element.209), kind=kOutput, calls=%fused_computation.16.clone.1 | convolution fusion | flops 216072192 | bytes 1835584 | tf_op jit(solution)/shard_map/while/body/eval_jaxpr/fbc,fdc->fbd/dot_general | solution.py:63
  1288.0 17.8 %fusion.140 = f32[9,16,32,128]{3,2,1,0:T(8,128)S(1)} fusion(f32[9,16,32,128]{3,2,1,0:T(8,128)S(1)} %get-tuple-element.222, s32[]{:T(128)} %get-tuple-element.220, f32[16,32,128]{2,1,0:T(8,128)S(1)} %fusion.139, s32[128,512]{1,0:T(8,128)S(1)} %get-tuple-element.235, s32[16]{0:T(128)S(1)} %iota_add_fusion.2, f32[16,32,512]{2,0,1:T(8,128)S(1)} %get-tuple-element.208), kind=kOutput, calls=%fused_computation.19.clone.1 | convolution fusion | flops 216072192 | bytes 1835524 | tf_op jit(solution)/shard_map/while/body/eval_jaxpr/fbc,fdc->fbd/dot_general | solution.py:66
  1323.1 18.6 %fusion.138 = f32[9,16,32,128]{3,2,1,0:T(8,128)} fusion(f32[9,16,32,128]{3,2,1,0:T(8,128)} %get-tuple-element.221, s32[]{:T(128)} %get-tuple-element.220, f32[16,32,128]{2,1,0:T(8,128)S(1)} %fusion.137, s32[128,512]{1,0:T(8,128)S(1)} %get-tuple-element.235, s32[16]{0:T(128)S(1)} %iota_add_fusion.2, f32[16,32,512]{2,0,1:T(8,128)S(1)} %get-tuple-element.209), kind=kOutput, calls=%fused_computation.16.clone.1 | convolution fusion | flops 216072192 | bytes 1835584 | tf_op jit(solution)/shard_map/while/body/eval_jaxpr/fbc,fdc->fbd/dot_general | solution.py:63
  1364.4 17.8 %fusion.140 = f32[9,16,32,128]{3,2,1,0:T(8,128)S(1)} fusion(f32[9,16,32,128]{3,2,1,0:T(8,128)S(1)} %get-tuple-element.222, s32[]{:T(128)} %get-tuple-element.220, f32[16,32,128]{2,1,0:T(8,128)S(1)} %fusion.139, s32[128,512]{1,0:T(8,128)S(1)} %get-tuple-element.235, s32[16]{0:T(128)S(1)} %iota_add_fusion.2, f32[16,32,512]{2,0,1:T(8,128)S(1)} %get-tuple-element.208), kind=kOutput, calls=%fused_computation.19.clone.1 | convolution fusion | flops 216072192 | bytes 1835524 | tf_op jit(solution)/shard_map/while/body/eval_jaxpr/fbc,fdc->fbd/dot_general | solution.py:66
  1399.6 18.6 %fusion.138 = f32[9,16,32,128]{3,2,1,0:T(8,128)} fusion(f32[9,16,32,128]{3,2,1,0:T(8,128)} %get-tuple-element.221, s32[]{:T(128)} %get-tuple-element.220, f32[16,32,128]{2,1,0:T(8,128)S(1)} %fusion.137, s32[128,512]{1,0:T(8,128)S(1)} %get-tuple-element.235, s32[16]{0:T(128)S(1)} %iota_add_fusion.2, f32[16,32,512]{2,0,1:T(8,128)S(1)} %get-tuple-element.209), kind=kOutput, calls=%fused_computation.16.clone.1 | convolution fusion | flops 216072192 | bytes 1835584 | tf_op jit(solution)/shard_map/while/body/eval_jaxpr/fbc,fdc->fbd/dot_general | solution.py:63
  (76 shorter events, 480.5 us)
Async XLA Ops:
  19.7 6.7 copy-start
  19.7 368.8 %all-to-all-start = ((bf16[2,32,16,32,256]{4,3,1,0,2:T(8,128)(2,1)}), bf16[2,32,16,32,256]{4,3,1,0,2:T(8,128)(2,1)}, u32[]{:S(2)}, u32[]{:S(2)}) async-start(bf16[2,32,16,32,256]{4,3,1,0,2:T(8,128)(2,1)} %copy.42), calls=%async_computation | async-start | bytes 33554432 | tf_op jit(solution)/shard_map/all_to_all | solution.py:103
  461.8 187.3 %all-to-all-start.1 = ((bf16[512,32,256]{2,1,0:T(8,128)(2,1)}), bf16[512,32,256]{2,1,0:T(8,128)(2,1)}, u32[]{:S(2)}, u32[]{:S(2)}) async-start(bf16[512,32,256]{2,1,0:T(8,128)(2,1)} %bitcast.58), calls=%async_computation.1 | async-start | bytes 16777216 | tf_op jit(solution)/shard_map/all_to_all | solution.py:105
  708.8 18.6 %copy-start.1 = (s32[128,512]{1,0:T(8,128)S(1)}, s32[128,512]{1,0:T(8,128)}, u32[]{:S(2)}) copy-start(s32[128,512]{1,0:T(8,128)} %param.9) | copy-start | bytes 786436
where the time goes:
time: 1450 us; the launch traced here: 1440 us
  matrix products  718 us (50%)
  waiting for transfers between devices  540 us (37%)
  local copies, waits for them, and re-layouts  76.5 us (5%)
  other arithmetic  66.3 us (5%)
  loops' own time  25.8 us (2%)
    all_to_all x1, waiting for transfers between devices, body(): lax.all_to_all(regrouped_in, 'chan', split_axis=2, concat_axis=1, tiled=T...  358 us
    all_to_all x1, waiting for transfers between devices, body(): lax.all_to_all(powers, 'chan', split_axis=0, concat_axis=1, tiled=True)  182 us
    dot_general x9, matrix products, spectrum(): jnp.einsum('fbc,fdc->fbd', part_imag, sin_rot, precision=precise)  167 us
    dot_general x9, matrix products, spectrum(): jnp.einsum('fbc,fdc->fbd', part_real, sin_rot, precision=precise)  160 us
    dot_general x9, matrix products, spectrum(): jnp.einsum('fbc,fdc->fbd', part_imag, cos_rot, precision=precise)  157 us
    dot_general x9, matrix products, spectrum(): jnp.einsum('fbc,fdc->fbd', part_real, cos_rot, precision=precise)  156 us
  transfers between devices with their start and end apart: 2, of which 2 were waited for; matrix products, arithmetic and copies ran while one was open for 0% of the time, Pallas kernels for 0%

commit v1 on v0

v1 whole, which is shorter than its diff:
```python
import functools
import math

import jax
import jax.numpy as jnp
import numpy as np
from jax import lax
from jax.experimental import pallas as pl
from jax.experimental.pallas import tpu as pltpu
from jax.sharding import PartitionSpec as P

PHASES = 1024
CHUNKS = 4


def beam_matrix(beam_phase, group_count, own_half):
    beam_count, station_count = beam_phase.shape
    half = group_count // 2
    local_beams = beam_count // group_count
    grid = beam_phase.reshape(2, half, local_beams, station_count)
    grid = jnp.where(own_half == 0, grid[::-1], grid)
    grid = jnp.transpose(grid, (1, 0, 2, 3)).reshape(beam_count, group_count, station_count // group_count)
    angles = grid.astype(jnp.float32) * (2.0 * math.pi / PHASES)
    scaling = 1.0 / math.sqrt(station_count)
    real_part = jnp.cos(angles) * scaling
    imag_part = jnp.sin(angles) * scaling
    upper_rows = jnp.stack([real_part, -imag_part], axis=2)
    bottom = jnp.stack([imag_part, real_part], axis=2)
    rows = jnp.concatenate([upper_rows, bottom], axis=0)
    return rows.reshape(2 * beam_count, 2 * station_count).astype(jnp.bfloat16)


def beam_kernel(weight_ref, table_ref, data_ref, out_ref):
    rows = weight_ref.shape[1]
    beams = weight_ref.shape[0] // 2
    data = data_ref[:, 0].reshape(rows, data_ref.shape[3])
    sums = jnp.dot(weight_ref[...], data, preferred_element_type=jnp.float32)
    powers = (sums[:beams] * sums[:beams] + sums[beams:] * sums[beams:]).astype(jnp.bfloat16)
    spectrum = jnp.dot(powers, table_ref[...], preferred_element_type=jnp.float32)
    out_ref[:, 0] = spectrum.astype(jnp.bfloat16).reshape(out_ref.shape[0], out_ref.shape[2], out_ref.shape[3])


def detect_spectra(weights, table, received):
    group_count, items, rows, time_count = received.shape
    beams = weights.shape[0] // 2
    half = group_count // 2
    return pl.pallas_call(
        beam_kernel,
        grid=(items,),
        out_shape=jax.ShapeDtypeStruct((half, items, beams // half, time_count), jnp.bfloat16),
        in_specs=[
            pl.BlockSpec(weights.shape, lambda c: (0, 0)),
            pl.BlockSpec(table.shape, lambda c: (0, 0)),
            pl.BlockSpec((group_count, 1, rows, time_count), lambda c: (0, c, 0, 0)),
        ],
        out_specs=pl.BlockSpec((half, 1, beams // half, time_count), lambda c: (0, c, 0, 0)),
        compiler_params=pltpu.CompilerParams(vmem_limit_bytes=32 * 2**20),
        cost_estimate=pl.CostEstimate(
            flops=2 * items * time_count * (weights.size + beams * time_count),
            bytes_accessed=2 * (received.size + weights.size + items * beams * time_count),
            transcendentals=0,
        ),
    )(weights, table, received)


def rotations(delays, time_count):
    freqs = time_count // 2
    low = min(16, freqs)
    high = freqs // low
    turned = delays.T

    def unit(multiples):
        level = multiples[:, None, None] * turned[None] % time_count
        angle = level.astype(jnp.float32) * (2.0 * math.pi / time_count)
        return jnp.cos(angle), jnp.sin(angle)

    low_cos, low_sin = unit(jnp.arange(1, low + 1, dtype=jnp.int32))
    high_cos, high_sin = unit(jnp.arange(high, dtype=jnp.int32) * low)
    cosine = high_cos[:, None] * low_cos[None] - high_sin[:, None] * low_sin[None]
    sine = high_cos[:, None] * low_sin[None] + high_sin[:, None] * low_cos[None]
    cosine = cosine.reshape((freqs,) + turned.shape).astype(jnp.bfloat16)
    sine = sine.reshape((freqs,) + turned.shape).astype(jnp.bfloat16)
    return jnp.concatenate(
        [jnp.concatenate([cosine, sine], axis=2), jnp.concatenate([-sine, cosine], axis=2)], axis=1
    )


def body(voltages, cal_gains, beam_phase, delays):
    group_count = lax.axis_size("chan")
    half = group_count // 2
    me = lax.axis_index("chan")
    own_half = me // half
    _, stations, channels, time_count = voltages.shape
    items = channels // group_count // CHUNKS
    freqs = time_count // 2
    trials = delays.shape[0]
    local_beams = beam_phase.shape[0] // group_count

    weights = beam_matrix(beam_phase, group_count, own_half)
    turn = np.outer(np.arange(time_count), np.arange(1, freqs + 1)) % time_count
    turn = turn * (2.0 * np.pi / time_count)
    table = jnp.asarray(np.concatenate([np.cos(turn), -np.sin(turn)], axis=1), jnp.bfloat16)
    share = np.where(np.arange(1, freqs + 1) == freqs, 1.0, 2.0)
    back = np.stack([np.cos(turn) * share, -np.sin(turn) * share], axis=0)
    back = jnp.asarray(back, jnp.bfloat16)

    gains = cal_gains.astype(jnp.float32) / 65536.0
    gains = gains.reshape(2, stations, group_count, CHUNKS, items)
    volts = voltages.reshape(2, stations, group_count, CHUNKS, items, time_count)
    groups = [list(range(half)), list(range(half, group_count))]
    arrived = []
    for k in range(CHUNKS):
        gain_real = gains[0, :, :, k, :, None]
        gain_imag = gains[1, :, :, k, :, None]
        volt_real = volts[0, :, :, k].astype(jnp.float32)
        volt_imag = volts[1, :, :, k].astype(jnp.float32)
        calibrated = jnp.stack(
            [
                volt_real * gain_real - volt_imag * gain_imag,
                volt_real * gain_imag + volt_imag * gain_real,
            ]
        ).astype(jnp.bfloat16)
        outgoing = jnp.transpose(calibrated, (2, 3, 0, 1, 4))
        outgoing = outgoing.reshape(group_count, items, 2 * stations, time_count)
        received = lax.all_to_all(outgoing, "chan", split_axis=0, concat_axis=0, tiled=True)
        spectra = detect_spectra(weights, table, received)
        arrived.append(
            lax.all_to_all(
                spectra, "chan", split_axis=0, concat_axis=0, tiled=True, axis_index_groups=groups
            )
        )
    picked = delays.reshape(trials, 2, half, CHUNKS, items)
    picked = lax.dynamic_index_in_dim(picked, own_half, axis=1, keepdims=False)
    order = jnp.transpose(picked, (0, 2, 1, 3)).reshape(trials, channels // 2)
    rotation = rotations(order, time_count)
    series = jnp.stack(arrived)
    series = series.reshape(channels // 2, 2, local_beams, 2, freqs)
    series = jnp.transpose(series, (1, 4, 2, 3, 0)).reshape(2, freqs, local_beams, channels)
    other = jnp.einsum("fbk,fkd->fbd", series[0], rotation, preferred_element_type=jnp.float32)
    pairs = [(i, (i + half) % group_count) for i in range(group_count)]
    incoming = lax.ppermute(other.astype(jnp.bfloat16), "chan", pairs)
    own = jnp.einsum("fbk,fkd->fbd", series[1], rotation, preferred_element_type=jnp.float32)
    total = (own + incoming.astype(jnp.float32)).astype(jnp.bfloat16)
    total = total.reshape(freqs, local_beams, 2, trials)
    result = jnp.einsum("fbpd,ptf->bdt", total, back, preferred_element_type=jnp.float32)
    return result * (1.0 / (time_count * math.sqrt(channels)))


def solution(mesh):
    return jax.shard_map(
        body,
        mesh=mesh,
        in_specs=(P(None, ("obs", "chan"), None, None), P(None, ("obs", "chan"), None), P(), P()),
        out_specs=P(("obs", "chan"), None, None),
        check_vma=False,
    )
```

time: 1450 us -> 743 us (0.51)
  matrix products: 718 us -> 34.7 us
  waiting for transfers between devices: 540 us -> 421 us
  Pallas kernels: 0 us -> 36.4 us
  starting transfers between devices: 11.6 us -> 47.4 us
  loops' own time: 25.8 us -> 0 us
  local copies, waits for them, and re-layouts: 76.5 us -> 101 us
  other arithmetic: 66.3 us -> 88.3 us
    dot_general x41 -> x3, matrix products: 718 us -> 34.7 us  [the longest x1 16.1 us: body(): jnp.einsum('fbk,fkd->fbd', series[0], rotation, preferred_element_type=jn...]
    all_to_all x2 -> x8, waiting for transfers between devices: 540 us -> 353 us  [the longest x4 312 us: body(): lax.all_to_all(outgoing, 'chan', split_axis=0, concat_axis=0, tiled=True)]
    ppermute x0 -> x1, waiting for transfers between devices: none -> 68 us  [body(): incoming = lax.ppermute(other.astype(jnp.bfloat16), 'chan', pairs)]
    slice x0 -> x4, local copies, waits for them, and re-layouts: none -> 51.9 us  [the longest x2 25.2 us: body(): series[1]]
    pallas_call x0 -> x4, Pallas kernels: none -> 36.4 us  [detect_spectra(): pl.pallas_call(beam_kernel, grid=(items,), out_shape=jax.ShapeDtypeStruct...]
    all_to_all x2 -> x8, starting transfers between devices: 11.6 us -> 44.4 us  [the longest x4 22.5 us: body(): lax.all_to_all(spectra, 'chan', split_axis=0, concat_axis=0, tiled=True,...]
    another operation x4, other arithmetic: 14.4 us -> 44.5 us
    dynamic_slice x18 -> x0, local copies, waits for them, and re-layouts: 25.8 us -> none  [the longest x9 20.1 us: spectrum(): part_imag = lax.dynamic_slice_in_dim(spec_imag, offset, fblock, 0)]
  transfers between devices with their start and end apart: 2 -> 9, of which waited for: 2 -> 8; matrix products, arithmetic and copies ran while one was open for 0% -> 13% of each run, Pallas kernels for 0% -> 5%
where the time goes in v1:
time: 743 us; the launch traced here: 730 us
  waiting for transfers between devices  421 us (57%)
  local copies, waits for them, and re-layouts  101 us (14%)
  other arithmetic  88.3 us (12%)
  starting transfers between devices  47.4 us (6%)
  Pallas kernels  36.4 us (5%)
  matrix products  34.7 us (5%)
    all_to_all x4, waiting for transfers between devices, body(): lax.all_to_all(outgoing, 'chan', split_axis=0, concat_axis=0, tiled=True)  312 us
    ppermute x1, waiting for transfers between devices, body(): incoming = lax.ppermute(other.astype(jnp.bfloat16), 'chan', pairs)  68 us
    all_to_all x4, waiting for transfers between devices, body(): lax.all_to_all(spectra, 'chan', split_axis=0, concat_axis=0, tiled=True,...  41 us
    another operation x3, other arithmetic  37.8 us
    pallas_call x4, Pallas kernels, detect_spectra(): pl.pallas_call(beam_kernel, grid=(items,), out_shape=jax.ShapeDtypeStruct...  36.4 us
    slice x2, local copies, waits for them, and re-layouts, body(): series[1]  25.2 us
    all_to_all x4, starting transfers between devices, body(): lax.all_to_all(spectra, 'chan', split_axis=0, concat_axis=0, tiled=True,...  22.5 us
    all_to_all x4, starting transfers between devices, body(): lax.all_to_all(outgoing, 'chan', split_axis=0, concat_axis=0, tiled=True)  21.9 us
  transfers between devices with their start and end apart: 9, of which 8 were waited for; matrix products, arithmetic and copies ran while one was open for 13% of the time, Pallas kernels for 5%

profile of v1, /device:TPU:13, one launch (start us, length us, event | category | flops | bytes accessed | tf_op | source)
XLA Modules:
  0.0 729.9 jit_solution(10888299033870184078)
XLA Ops:
  0.0 11.7 %fusion.37 = (bf16[1,32,16,1,8,256]{5,4,3,2,1,0:T(8,128)(2,1)}, bf16[1,32,16,1,8,256]{5,4,3,2,1,0:T(8,128)(2,1)S(1)}, bf16[1,32,16,1,8,256]{5,4,3,2,1,0:T(8,128)...) fusion(bf16[2,32,16,4,8,256]{5,4,3,2,1,0:T(8,128)(2,1)} %bitcas, ...), kind=kLoop, calls=%fused_computation.99 | loop fusion | bytes 33554432 | tf_op jit(solution)/shard_map/slice | solution.py:116
  12.0 17.8 %fusion.3 = (bf16[1,32,16,8,256]{4,1,0,3,2:T(8,128)(2,1)S(1)}, bf16[1,32,16,8,256]{4,1,0,3,2:T(8,128)(2,1)S(1)}, bf16[1,32,16,8,256]{4,1,0,3,2:T(8,128)(2,1)}, bf16[1,32,16,8,256]{4,1,0,3,2:T(8,128)(2,1)}) fusion(f32[32,16,8]{0,2,1:T(8,128)S(1)} %get-tuple-element.35, f32[32,16,8]{0,2,1:T(8,128)S(1)} %get-tuple-element.28, ...), kind=kLoop, calls=%fused_computation.23 | loop fusion | flops 20971520 | bytes 16842752 | tf_op jit(solution)/shard_map/convert.14
  43.3 87.8 %all-to-all-done.data_ref = bf16[16,8,64,256]{3,2,1,0:T(8,128)(2,1)} async-done(((bf16[16,8,64,256]{3,2,1,0:T(8,128)(2,1)}), bf16[16,8,64,256]{3,2,1,0:T(8,128)(2,1)}, u32[]{:S(2)}, u32[]{:S(2)}) %all-to-all-start) | async-done | bytes 4194336 | tf_op jit(solution)/shard_map/all_to_all | solution.py:125
  136.1 15.4 %fusion.11 = (bf16[1,32,16,8,256]{4,1,0,3,2:T(8,128)(2,1)S(1)}, bf16[1,32,16,8,256]{4,1,0,3,2:T(8,128)(2,1)S(1)}, bf16[1,32,16,8,256]{4,1,0,3,2:T(8,128)(2,1)}, bf16[1,32,16,8,256]{4,1,0,3,2:T(8,128)(2,1)}) fusion(f32[32,16,8]{0,2,1:T(8,128)S(1)} %get-tuple-element.31, f32[32,16,8]{0,2,1:T(8,128)S(1)} %get-tuple-element.32, ...), kind=kLoop, calls=%fused_computation.31 | loop fusion | flops 20971520 | bytes 16842752 | tf_op jit(solution)/shard_map/convert.10
  153.8 74.8 %all-to-all-done.2.data_ref = bf16[16,8,64,256]{3,2,1,0:T(8,128)(2,1)} async-done(((bf16[16,8,64,256]{3,2,1,0:T(8,128)(2,1)}), bf16[16,8,64,256]{3,2,1,0:T(8,128)(2,1)}, u32[]{:S(2)}, u32[]{:S(2)}) %all-to-all-start.2) | async-done | bytes 4194336 | tf_op jit(solution)/shard_map/all_to_all | solution.py:125
  237.6 88.5 %all-to-all-done.4.data_ref = bf16[16,8,64,256]{3,2,1,0:T(8,128)(2,1)} async-done(((bf16[16,8,64,256]{3,2,1,0:T(8,128)(2,1)}), bf16[16,8,64,256]{3,2,1,0:T(8,128)(2,1)}, u32[]{:S(2)}, u32[]{:S(2)}) %all-to-all-start.4) | async-done | bytes 4194336 | tf_op jit(solution)/shard_map/all_to_all | solution.py:125
  352.5 8.8 %shard_map.64 = bf16[8,8,64,256]{3,2,1,0:T(8,128)(2,1)S(1)} custom-call(bf16[1024,1024]{1,0:T(8,128)(2,1)S(1)} %copy.103.weight_ref, bf16[256,256]{1,0:T(8,128)(2,1)S(1)} %copy-done.3, bf16[16,8,64,256]{3,2,1,0:T(8,128)(2,1)} %all-to-all-done.data_ref), custom_call_target="tpu_custom_call" | custom-call | flops 4831838208 | bytes 8388608 | tf_op jit(solution)/shard_map/pallas_call | solution.py:47
  362.8 61.0 %all-to-all-done.6.data_ref = bf16[16,8,64,256]{3,2,1,0:T(8,128)(2,1)} async-done(((bf16[16,8,64,256]{3,2,1,0:T(8,128)(2,1)}), bf16[16,8,64,256]{3,2,1,0:T(8,128)(2,1)}, u32[]{:S(2)}, u32[]{:S(2)}) %all-to-all-start.6) | async-done | bytes 4194336 | tf_op jit(solution)/shard_map/all_to_all | solution.py:125
  428.1 8.8 %shard_map.65 = bf16[8,8,64,256]{3,2,1,0:T(8,128)(2,1)S(1)} custom-call(bf16[1024,1024]{1,0:T(8,128)(2,1)S(1)} %copy.103.weight_ref, bf16[256,256]{1,0:T(8,128)(2,1)S(1)} %copy-done.3, bf16[16,8,64,256]{3,2,1,0:T(8,128)(2,1)} %all-to-all-done.2.data_ref), custom_call_target="tpu_custom_call" | custom-call | flops 4831838208 | bytes 8388608 | tf_op jit(solution)/shard_map/pallas_call | solution.py:47
  438.2 13.4 %all-to-all-done.1 = bf16[8,8,64,256]{3,2,1,0:T(8,128)(2,1)} async-done(((bf16[8,8,64,256]{3,2,1,0:T(8,128)(2,1)}), bf16[8,8,64,256]{3,2,1,0:T(8,128)(2,1)}, u32[]{:S(2)}, u32[]{:S(2)}) %all-to-all-start.1) | async-done | bytes 2097184 | tf_op jit(solution)/shard_map/all_to_all | solution.py:128
  457.9 8.8 %shard_map.66 = bf16[8,8,64,256]{3,2,1,0:T(8,128)(2,1)S(1)} custom-call(bf16[1024,1024]{1,0:T(8,128)(2,1)S(1)} %copy.103.weight_ref, bf16[256,256]{1,0:T(8,128)(2,1)S(1)} %copy-done.3, bf16[16,8,64,256]{3,2,1,0:T(8,128)(2,1)} %all-to-all-done.4.data_ref), custom_call_target="tpu_custom_call" | custom-call | flops 4831838208 | bytes 8388608 | tf_op jit(solution)/shard_map/pallas_call | solution.py:47
  468.1 13.6 %all-to-all-done.3 = bf16[8,8,64,256]{3,2,1,0:T(8,128)(2,1)} async-done(((bf16[8,8,64,256]{3,2,1,0:T(8,128)(2,1)}), bf16[8,8,64,256]{3,2,1,0:T(8,128)(2,1)}, u32[]{:S(2)}, u32[]{:S(2)}) %all-to-all-start.3) | async-done | bytes 2097184 | tf_op jit(solution)/shard_map/all_to_all | solution.py:128
  487.9 9.8 %shard_map.67 = bf16[8,8,64,256]{3,2,1,0:T(8,128)(2,1)} custom-call(bf16[1024,1024]{1,0:T(8,128)(2,1)S(1)} %copy.103.weight_ref, bf16[256,256]{1,0:T(8,128)(2,1)S(1)} %copy-done.3, bf16[16,8,64,256]{3,2,1,0:T(8,128)(2,1)} %all-to-all-done.6.data_ref), custom_call_target="tpu_custom_call" | custom-call | flops 4831838208 | bytes 8388608 | tf_op jit(solution)/shard_map/pallas_call | solution.py:47
  497.8 14.0 %all-to-all-done.5 = bf16[8,8,64,256]{3,2,1,0:T(8,128)(2,1)} async-done(((bf16[8,8,64,256]{3,2,1,0:T(8,128)(2,1)}), bf16[8,8,64,256]{3,2,1,0:T(8,128)(2,1)}, u32[]{:S(2)}, u32[]{:S(2)}) %all-to-all-start.5) | async-done | bytes 2097184 | tf_op jit(solution)/shard_map/all_to_all | solution.py:128
  521.8 8.4 %fusion.28 = (f32[16,256,128]{2,1,0:T(8,128)S(1)}, f32[16,256,128]{2,1,0:T(8,128)S(1)}) fusion(s32[256,128]{1,0:T(8,128)S(1)} %bitcast.142, s32[16]{0:T(128)S(1)} %iota_add_fusion), kind=kLoop, calls=%fused_computation.76 | loop fusion | flops 7340032 | bytes 4325440 | tf_op jit(solution)/shard_map/cos | solution.py:75
  537.8 7.7 %bitcast_negate_fusion = bf16[128,256,128]{2,1,0:T(8,128)(2,1)} fusion(bf16[8,16,256,128]{3,2,1,0:T(8,128)(2,1)} %get-tuple-element.15), kind=kLoop, calls=%fused_computation.98 | loop fusion | flops 4194304 | bytes 16777216 | tf_op jit(solution)/shard_map/neg | solution.py:84
  552.2 12.5 %reshape.362 = bf16[256,2,32,2,128]{4,3,2,1,0:T(2,128)(2,1)} reshape(bf16[4,8,8,64,256]{4,3,2,1,0:T(8,128)(2,1)} %pad_maximum_fusion) | data formatting | bytes 16777216 | tf_op jit(solution)/shard_map/reshape | solution.py:137
  564.7 10.2 %fusion.38 = (bf16[1,128,32,2,256]{1,3,2,0,4:T(2,128)(2,1)}, bf16[1,128,32,2,256]{1,3,2,0,4:T(2,128)(2,1)}) fusion(bf16[2,128,32,2,256]{1,3,2,0,4:T(2,128)(2,1)} %bitcast.127), kind=kLoop, calls=%fused_computation.100 | loop fusion | bytes 16777216 | tf_op jit(solution)/shard_map/slice | solution.py:142
  574.9 15.0 %copy.116 = bf16[1,128,32,2,256]{4,3,2,1,0:T(2,128)(2,1)} copy(bf16[1,128,32,2,256]{1,3,2,0,4:T(2,128)(2,1)} %get-tuple-element.14) | data formatting | bytes 8388608 | tf_op jit(solution)/shard_map/slice | solution.py:139
  589.9 7.7 %squeeze.10 = bf16[128,32,512]{2,1,0:T(8,128)(2,1)} reshape(bf16[1,128,32,2,256]{4,3,2,1,0:T(2,128)(2,1)} %copy.116) | data formatting | bytes 8388608 | tf_op jit(solution)/shard_map/squeeze | solution.py:139
  597.6 16.1 %fusion.21 = bf16[128,32,256]{2,1,0:T(8,128)(2,1)} fusion(bf16[128,32,512]{2,1,0:T(8,128)(2,1)} %squeeze.10, bf16[128,256,128]{2,1,0:T(8,128)(2,1)} %bitcast.137, bf16[128,256,128]{2,1,0:T(8,128)(2,1)} %bitcast_negate_fusion, bf16[128,256,128]{2,1,0:T(8,128)(2,1)} %bitcast.128), kind=kOutput, calls=%fused_computation.64 | convolution fusion | flops 1209008128 | bytes 31457280 | tf_op jit(solution)/shard_map/fbk,fkd->fbd/dot_general | solution.py:139
  616.7 15.0 %copy.113 = bf16[1,128,32,2,256]{4,3,2,1,0:T(2,128)(2,1)} copy(bf16[1,128,32,2,256]{1,3,2,0,4:T(2,128)(2,1)} %get-tuple-element.13) | data formatting | bytes 8388608 | tf_op jit(solution)/shard_map/slice | solution.py:142
  639.3 68.0 %collective-permute-done = bf16[128,32,256]{2,1,0:T(8,128)(2,1)S(1)} collective-permute-done((bf16[128,32,256]{2,1,0:T(8,128)(2,1)}, bf16[128,32,256]{2,1,0:T(8,128)(2,1)S(1)}, u32[]{:S(2)}, u32[]{:S(2)}) %collective-permute-start) | collective-permute-done | bytes 2097184 | tf_op jit(solution)/shard_map/ppermute | solution.py:141
  707.3 15.9 %add_convert_fusion.1 = bf16[128,32,256]{2,1,0:T(8,128)(2,1)} fusion(bf16[128,32,256]{2,1,0:T(8,128)(2,1)S(1)} %collective-permute-done, bf16[128,32,512]{2,1,0:T(8,128)(2,1)} %squeeze.7, bf16[128,256,128]{2,1,0:T(8,128)(2,1)} %bitcast.138, bf16[128,256,128]{2,1,0:T(8,128)(2,1)} %bitcast_negate_fusion, bf16[128,256,128]{2,1,0:T(8,128)(2,1)} %bitcast.129), kind=kOutput, calls=%fused_computation.43 | convolution fusion | flops 1211105280 | bytes 33554432 | tf_op jit(solution)/shard_map/fbk,fkd->fbd/dot_general | solution.py:142
  (56 shorter events, 118.4 us)
Async XLA Ops:
  0.0 11.7 %copy-start.8 = (s32[2,32,512]{2,1,0:T(8,128)S(1)}, s32[2,32,512]{2,1,0:T(8,128)}, u32[]{:S(2)}) copy-start(s32[2,32,512]{2,1,0:T(8,128)} %param.7) | copy-start | bytes 393220
  32.2 99.0 %all-to-all-start = ((bf16[16,8,64,256]{3,2,1,0:T(8,128)(2,1)}), bf16[16,8,64,256]{3,2,1,0:T(8,128)(2,1)}, u32[]{:S(2)}, u32[]{:S(2)}) async-start(bf16[16,8,64,256]{3,2,1,0:T(8,128)(2,1)} %bitcast.134), calls=%async_computation | async-start | bytes 8388608 | tf_op jit(solution)/shard_map/all_to_all | solution.py:125
  131.2 97.4 %all-to-all-start.2 = ((bf16[16,8,64,256]{3,2,1,0:T(8,128)(2,1)}), bf16[16,8,64,256]{3,2,1,0:T(8,128)(2,1)}, u32[]{:S(2)}, u32[]{:S(2)}) async-start(bf16[16,8,64,256]{3,2,1,0:T(8,128)(2,1)} %bitcast.132), calls=%async_computation.2 | async-start | bytes 8388608 | tf_op jit(solution)/shard_map/all_to_all | solution.py:125
  228.6 5.0 copy-start.4
  228.6 97.5 %all-to-all-start.4 = ((bf16[16,8,64,256]{3,2,1,0:T(8,128)(2,1)}), bf16[16,8,64,256]{3,2,1,0:T(8,128)(2,1)}, u32[]{:S(2)}, u32[]{:S(2)}) async-start(bf16[16,8,64,256]{3,2,1,0:T(8,128)(2,1)} %bitcast.133), calls=%async_computation.4 | async-start | bytes 8388608 | tf_op jit(solution)/shard_map/all_to_all | solution.py:125
  326.1 5.4 copy-start.5
  326.1 97.7 %all-to-all-start.6 = ((bf16[16,8,64,256]{3,2,1,0:T(8,128)(2,1)}), bf16[16,8,64,256]{3,2,1,0:T(8,128)(2,1)}, u32[]{:S(2)}, u32[]{:S(2)}) async-start(bf16[16,8,64,256]{3,2,1,0:T(8,128)(2,1)} %bitcast.131), calls=%async_computation.6 | async-start | bytes 8388608 | tf_op jit(solution)/shard_map/all_to_all | solution.py:125
  347.0 5.6 copy-start.3
  361.4 1.4 copy-start.1
  423.8 27.9 %all-to-all-start.1 = ((bf16[8,8,64,256]{3,2,1,0:T(8,128)(2,1)}), bf16[8,8,64,256]{3,2,1,0:T(8,128)(2,1)}, u32[]{:S(2)}, u32[]{:S(2)}) async-start(bf16[8,8,64,256]{3,2,1,0:T(8,128)(2,1)} %copy-done.1), calls=%async_computation.1 | async-start | bytes 4194304 | tf_op jit(solution)/shard_map/all_to_all | solution.py:128
  436.9 1.3 copy-start.2
  451.6 30.0 %all-to-all-start.3 = ((bf16[8,8,64,256]{3,2,1,0:T(8,128)(2,1)}), bf16[8,8,64,256]{3,2,1,0:T(8,128)(2,1)}, u32[]{:S(2)}, u32[]{:S(2)}) async-start(bf16[8,8,64,256]{3,2,1,0:T(8,128)(2,1)} %copy-done.2), calls=%async_computation.3 | async-start | bytes 4194304 | tf_op jit(solution)/shard_map/all_to_all | solution.py:128
  466.7 1.4 copy-start
  481.7 30.0 %all-to-all-start.5 = ((bf16[8,8,64,256]{3,2,1,0:T(8,128)(2,1)}), bf16[8,8,64,256]{3,2,1,0:T(8,128)(2,1)}, u32[]{:S(2)}, u32[]{:S(2)}) async-start(bf16[8,8,64,256]{3,2,1,0:T(8,128)(2,1)} %copy-done), calls=%async_computation.5 | async-start | bytes 4194304 | tf_op jit(solution)/shard_map/all_to_all | solution.py:128
  497.8 19.7 %copy-start.6 = (s32[128,512]{1,0:T(8,128)S(1)}, s32[128,512]{1,0:T(8,128)}, u32[]{:S(2)}) copy-start(s32[128,512]{1,0:T(8,128)} %param.9) | copy-start | bytes 786436
  511.7 33.8 %all-to-all-start.7 = ((bf16[8,8,64,256]{3,2,1,0:T(8,128)(2,1)}), bf16[8,8,64,256]{3,2,1,0:T(8,128)(2,1)S(1)}, u32[]{:S(2)}, u32[]{:S(2)}) async-start(bf16[8,8,64,256]{3,2,1,0:T(8,128)(2,1)} %shard_map.67), calls=%async_computation.7 | async-start | bytes 4194304 | tf_op jit(solution)/shard_map/all_to_all | solution.py:128
  613.7 93.6 %collective-permute-start = (bf16[128,32,256]{2,1,0:T(8,128)(2,1)}, bf16[128,32,256]{2,1,0:T(8,128)(2,1)S(1)}, u32[]{:S(2)}, u32[]{:S(2)}) collective-permute-start(bf16[128,32,256]{2,1,0:T(8,128)(2,1)} %fusion.21), channel_id=1, source_target_pairs={{0,8},{1,9},{2,10},{3,11},{4,12},{5,13},{6,14},{7,15},{8,0},{9,1},... | collective-permute-start | bytes 6291464 | tf_op jit(solution)/shard_map/ppermute | solution.py:141
  723.2 3.5 copy-start.7

commit v2 on v1

v2 whole, which is shorter than its diff:
```python
import functools
import math

import jax
import jax.numpy as jnp
import numpy as np
from jax import lax
from jax.experimental import pallas as pl
from jax.experimental.pallas import tpu as pltpu
from jax.sharding import PartitionSpec as P

PHASES = 1024
CHUNKS = 4


def beam_matrix(beam_phase, group_count, own_half):
    beam_count, station_count = beam_phase.shape
    half = group_count // 2
    local_beams = beam_count // group_count
    grid = beam_phase.reshape(2, half, local_beams, station_count)
    grid = jnp.where(own_half == 0, grid[::-1], grid)
    grid = jnp.transpose(grid, (1, 0, 2, 3)).reshape(beam_count, group_count, station_count // group_count)
    angles = grid.astype(jnp.float32) * (2.0 * math.pi / PHASES)
    scaling = 1.0 / math.sqrt(station_count)
    real_part = jnp.cos(angles) * scaling
    imag_part = jnp.sin(angles) * scaling
    upper_rows = jnp.stack([real_part, -imag_part], axis=2)
    bottom = jnp.stack([imag_part, real_part], axis=2)
    rows = jnp.concatenate([upper_rows, bottom], axis=0)
    return rows.reshape(2 * beam_count, 2 * station_count).astype(jnp.bfloat16)


def exchange_kernel(
    count, items, data_ref, weight_ref, table_ref, out_ref, held, spectra, send_in, recv_in, send_out, recv_out, local_in, local_out
):
    me = lax.axis_index("chan")
    half = count // 2
    first = me // half * half
    place = lax.rem(me, half)
    channels = data_ref.shape[1]
    chunks = channels // items
    beams = weight_ref.shape[0] // 2

    barrier = pltpu.get_barrier_semaphore()

    def greet(step, carry):
        pl.semaphore_signal(
            barrier, inc=1, device_id={"chan": lax.rem(me + step, count)}, device_id_type=pl.DeviceIdType.MESH
        )
        return carry

    lax.fori_loop(1, count, greet, 0)
    pl.semaphore_wait(barrier, count - 1)

    def inward(k, step):
        target = lax.rem(me + step, count)
        part = pl.ds(k * items, items)
        return pltpu.make_async_remote_copy(
            src_ref=data_ref.at[target, part],
            dst_ref=held.at[me, part],
            send_sem=send_in.at[k, step],
            recv_sem=recv_in.at[k, step],
            device_id={"chan": target},
            device_id_type=pl.DeviceIdType.MESH,
        )

    def outward(k, step):
        target = lax.rem(place + step, half)
        part = pl.ds(k * items, items)
        return pltpu.make_async_remote_copy(
            src_ref=spectra.at[target, part],
            dst_ref=out_ref.at[place, part],
            send_sem=send_out.at[k, step],
            recv_sem=recv_out.at[k, step],
            device_id={"chan": first + target},
            device_id_type=pl.DeviceIdType.MESH,
        )

    def each(start, stop, act):
        def run(step, carry):
            act(step)
            return carry

        lax.fori_loop(start, stop, run, 0)

    own = pltpu.make_async_copy(data_ref.at[me], held.at[me], local_in)
    ahead = 2
    for k in range(min(ahead, chunks)):
        each(1, count, lambda step: inward(k, step).start())
    own.start()
    own.wait()
    for k in range(chunks):
        each(1, count, lambda step: inward(k, step).wait_recv())
        if k + ahead < chunks:
            each(1, count, lambda step: inward(k + ahead, step).start())

        def channel(c):
            data = held[:, c].reshape(weight_ref.shape[1], held.shape[3])
            sums = jnp.dot(weight_ref[...], data, preferred_element_type=jnp.float32)
            powers = (sums[:beams] * sums[:beams] + sums[beams:] * sums[beams:]).astype(jnp.bfloat16)
            series = jnp.dot(powers, table_ref[...], preferred_element_type=jnp.float32)
            spectra[:, c] = series.astype(jnp.bfloat16).reshape(half, spectra.shape[2], spectra.shape[3])

        each(k * items, (k + 1) * items, channel)
        each(1, half, lambda step: outward(k, step).start())
    stay = pltpu.make_async_copy(spectra.at[place], out_ref.at[place], local_out)
    stay.start()
    stay.wait()
    for k in range(chunks):
        each(1, count, lambda step: inward(k, step).wait_send())
        each(1, half, lambda step: outward(k, step).wait())


def exchange(weights, table, data):
    count, channels, rows, time_count = data.shape
    beams = weights.shape[0] // 2
    half = count // 2
    found = (half, channels, beams // half, time_count)
    return pl.pallas_call(
        functools.partial(exchange_kernel, count, channels // CHUNKS),
        out_shape=jax.ShapeDtypeStruct(found, jnp.bfloat16),
        in_specs=[
            pl.BlockSpec(memory_space=pl.ANY),
            pl.BlockSpec(memory_space=pltpu.VMEM),
            pl.BlockSpec(memory_space=pltpu.VMEM),
        ],
        out_specs=pl.BlockSpec(memory_space=pl.ANY),
        scratch_shapes=[
            pltpu.VMEM(data.shape, jnp.bfloat16),
            pltpu.VMEM(found, jnp.bfloat16),
            pltpu.SemaphoreType.DMA((CHUNKS, count)),
            pltpu.SemaphoreType.DMA((CHUNKS, count)),
            pltpu.SemaphoreType.DMA((CHUNKS, half)),
            pltpu.SemaphoreType.DMA((CHUNKS, half)),
            pltpu.SemaphoreType.DMA,
            pltpu.SemaphoreType.DMA,
        ],
        compiler_params=pltpu.CompilerParams(
            collective_id=0, has_side_effects=True, vmem_limit_bytes=48 * 2**20
        ),
        cost_estimate=pl.CostEstimate(
            flops=2 * channels * time_count * (weights.size + beams * time_count),
            bytes_accessed=4 * data.size,
            transcendentals=0,
        ),
    )(data, weights, table)


def rotations(delays, time_count):
    freqs = time_count // 2
    low = min(16, freqs)
    high = freqs // low
    turned = delays.T

    def unit(multiples):
        level = multiples[:, None, None] * turned[None] % time_count
        angle = level.astype(jnp.float32) * (2.0 * math.pi / time_count)
        return jnp.cos(angle), jnp.sin(angle)

    low_cos, low_sin = unit(jnp.arange(1, low + 1, dtype=jnp.int32))
    high_cos, high_sin = unit(jnp.arange(high, dtype=jnp.int32) * low)
    cosine = high_cos[:, None] * low_cos[None] - high_sin[:, None] * low_sin[None]
    sine = high_cos[:, None] * low_sin[None] + high_sin[:, None] * low_cos[None]
    cosine = cosine.reshape((freqs,) + turned.shape).astype(jnp.bfloat16)
    sine = sine.reshape((freqs,) + turned.shape).astype(jnp.bfloat16)
    return jnp.concatenate([cosine, sine], axis=2)


def rotate(series, rotation, trials):
    channels, beams, samples = series.shape
    freqs = samples // 2
    series = series.reshape(channels, beams, 2, freqs)
    series = jnp.transpose(series, (3, 2, 1, 0)).reshape(freqs, 2 * beams, channels)
    parts = jnp.einsum("frk,fkd->frd", series, rotation, preferred_element_type=jnp.float32)
    real_part = parts[:, :beams, :trials] - parts[:, beams:, trials:]
    imag_part = parts[:, :beams, trials:] + parts[:, beams:, :trials]
    return jnp.concatenate([real_part, imag_part], axis=2)


def body(voltages, cal_gains, beam_phase, delays):
    group_count = lax.axis_size("chan")
    half = group_count // 2
    me = lax.axis_index("chan")
    own_half = me // half
    _, stations, channels, time_count = voltages.shape
    freqs = time_count // 2
    trials = delays.shape[0]
    local_beams = beam_phase.shape[0] // group_count

    weights = beam_matrix(beam_phase, group_count, own_half)
    turn = np.outer(np.arange(time_count), np.arange(1, freqs + 1)) % time_count
    turn = turn * (2.0 * np.pi / time_count)
    table = jnp.asarray(np.concatenate([np.cos(turn), -np.sin(turn)], axis=1), jnp.bfloat16)
    share = np.where(np.arange(1, freqs + 1) == freqs, 1.0, 2.0)
    back = np.stack([np.cos(turn) * share, -np.sin(turn) * share], axis=0)
    back = jnp.asarray(back, jnp.bfloat16)

    gains = cal_gains.astype(jnp.float32) / 65536.0
    gain_real = gains[0][:, :, None]
    gain_imag = gains[1][:, :, None]
    volt_real = voltages[0].astype(jnp.float32)
    volt_imag = voltages[1].astype(jnp.float32)
    calibrated = jnp.stack(
        [
            volt_real * gain_real - volt_imag * gain_imag,
            volt_real * gain_imag + volt_imag * gain_real,
        ]
    ).astype(jnp.bfloat16)
    outgoing = jnp.transpose(calibrated.reshape(2 * stations, channels, time_count), (1, 0, 2))
    outgoing = outgoing.reshape(group_count, channels // group_count, 2 * stations, time_count)
    arrived = exchange(weights, table, outgoing)

    order = delays.reshape(trials, 2, channels // 2)
    order = lax.dynamic_index_in_dim(order, own_half, axis=1, keepdims=False)
    rotation = rotations(order, time_count)
    series = arrived.reshape(channels // 2, 2 * local_beams, time_count)
    other = rotate(series[:, :local_beams], rotation, trials)
    pairs = [(i, (i + half) % group_count) for i in range(group_count)]
    incoming = lax.ppermute(other.astype(jnp.bfloat16), "chan", pairs)
    own = lax.optimization_barrier(rotate(series[:, local_beams:], rotation, trials))
    total = (own + incoming.astype(jnp.float32)).astype(jnp.bfloat16)
    total = total.reshape(freqs, local_beams, 2, trials)
    result = jnp.einsum("fbpd,ptf->bdt", total, back, preferred_element_type=jnp.float32)
    return result * (1.0 / (time_count * math.sqrt(channels)))


def solution(mesh):
    return jax.shard_map(
        body,
        mesh=mesh,
        in_specs=(P(None, ("obs", "chan"), None, None), P(None, ("obs", "chan"), None), P(), P()),
        out_specs=P(("obs", "chan"), None, None),
        check_vma=False,
    )
```

time: 743 us -> 640 us (0.86)
  Pallas kernels: 36.4 us -> 414 us
  waiting for transfers between devices: 421 us -> 52.4 us
  starting transfers between devices: 47.4 us -> 0.07 us
  other arithmetic: 88.3 us -> 57.4 us
  local copies, waits for them, and re-layouts: 101 us -> 81.6 us
    pallas_call x4 -> x1, Pallas kernels: 36.4 us -> 414 us  [exchange(): pl.pallas_call(functools.partial(exchange_kernel, count, channels // CHUN...]
    all_to_all x8 -> x0, waiting for transfers between devices: 353 us -> none  [the longest x4 312 us: body(): lax.all_to_all(outgoing, 'chan', split_axis=0, concat_axis=0, tiled=True)]
    slice x4 -> x1, local copies, waits for them, and re-layouts: 51.9 us -> 6.11 us  [body(): other = rotate(series[:, :local_beams], rotation, trials)]
    all_to_all x8 -> x0, starting transfers between devices: 44.4 us -> none  [the longest x4 22.5 us: body(): lax.all_to_all(spectra, 'chan', split_axis=0, concat_axis=0, tiled=True,...]
    convert_element_type x0 -> x1, local copies, waits for them, and re-layouts: none -> 26.4 us  [body(): calibrated = jnp.stack([volt_real * gain_real - volt_imag * gain_imag, vo...]
    another operation x4 -> x3, other arithmetic: 44.5 us -> 19.7 us
    reshape x1 -> x4, local copies, waits for them, and re-layouts: 12.5 us -> 31.8 us  [rotate(): series = series.reshape(channels, beams, 2, freqs)]
    ppermute x1, waiting for transfers between devices: 68 us -> 52.4 us  [body(): incoming = lax.ppermute(other.astype(jnp.bfloat16), 'chan', pairs)]
  transfers between devices with their start and end apart: 9 -> 1, of which waited for: 8 -> 1; matrix products, arithmetic and copies ran while one was open for 13% -> 5% of each run, Pallas kernels for 5% -> 0%
where the time goes in v2:
time: 640 us; the launch traced here: 634 us
  Pallas kernels  414 us (65%)
  local copies, waits for them, and re-layouts  81.6 us (13%)
  other arithmetic  57.4 us (9%)
  waiting for transfers between devices  52.4 us (8%)
  matrix products  28 us (4%)
    pallas_call x1, Pallas kernels, exchange(): pl.pallas_call(functools.partial(exchange_kernel, count, channels // CHUN...  414 us
    ppermute x1, waiting for transfers between devices, body(): incoming = lax.ppermute(other.astype(jnp.bfloat16), 'chan', pairs)  52.4 us
    reshape x4, local copies, waits for them, and re-layouts, rotate(): series = series.reshape(channels, beams, 2, freqs)  31.8 us
    convert_element_type x1, local copies, waits for them, and re-layouts, body(): calibrated = jnp.stack([volt_real * gain_real - volt_imag * gain_imag, vo...  26.4 us
    dot_general x2, matrix products, rotate(): jnp.einsum('frk,fkd->frd', series, rotation, preferred_element_type=jnp.f...  25.2 us
    another operation x3, other arithmetic  19.7 us
    cos x2, other arithmetic, unit(): return (jnp.cos(angle), jnp.sin(angle))  14.4 us
  transfers between devices with their start and end apart: 1, of which 1 were waited for; matrix products, arithmetic and copies ran while one was open for 5% of the time, Pallas kernels for 0%

profile of v2, /device:TPU:13, one launch (start us, length us, event | category | flops | bytes accessed | tf_op | source)
XLA Modules:
  0.0 633.9 jit_solution(4412706481653611873)
XLA Ops:
  0.9 10.5 %fusion.1 = (bf16[1,32,512,256]{3,2,1,0:T(8,128)(2,1)S(1)}, bf16[1,32,512,256]{3,2,1,0:T(8,128)(2,1)S(1)}) fusion(f32[32,512]{1,0:T(8,128)S(1)} %get-tuple-element.23, f32[32,512]{1,0:T(8,128)S(1)} %get-tuple-element.22, bf16[2,32,512,256]{3,2,1,0:T(8,128)(2,1)} %param.6), kind=kLoop, calls=%fused_computation.5 | loop fusion | flops 41943040 | bytes 33685504 | tf_op jit(solution)/shard_map/convert.8
  13.1 26.4 %copy.36 = bf16[64,512,256]{2,0,1:T(8,128)(2,1)} copy(bf16[64,512,256]{2,1,0:T(8,128)(2,1)S(1)} %bitcast.47) | data formatting | bytes 33554432 | tf_op jit(solution)/shard_map/convert_element_type | solution.py:208
  39.6 4.6 fusion.21
  49.9 2.7 reshape.153
  52.6 2.3 copy.40
  54.9 2.7 maximum_maximum_fusion
  57.6 2.9 copy.43.weight_ref
  60.5 414.3 %shard_map.64 = bf16[8,32,64,256]{3,2,1,0:T(8,128)(2,1)} custom-call(bf16[16,32,64,256]{3,2,1,0:T(8,128)(2,1)} %bitcast.48, bf16[1024,1024]{1,0:T(8,128)(2,1)S(1)} %copy.43.weight_ref, bf16[256,256]{1,0:T(8,128)(2,1)S(1)} %copy-done), custom_call_target="tpu_custom_call" | custom-call | flops 19327352832 | bytes 33554432 | tf_op jit(solution)/shard_map/pallas_call | solution.py:119
  474.8 6.1 fusion.26
  481.1 9.3 %fusion.17 = (f32[16,256,128]{2,1,0:T(8,128)S(1)}, f32[16,256,128]{2,1,0:T(8,128)}) fusion(s32[256,128]{1,0:T(8,128)S(1)} %dynamic-slice_bitcast_fusion, s32[16]{0:T(128)S(1)} %iota_add_fusion), kind=kLoop, calls=%fused_computation.47 | loop fusion | flops 7340032 | bytes 4325440 | tf_op jit(solution)/shard_map/cos | solution.py:158
  490.3 5.1 fusion.23
  495.5 6.9 %reshape.147 = bf16[256,32,2,128]{3,2,1,0:T(2,128)(2,1)} reshape(bf16[256,32,256]{2,1,0:T(8,128)(2,1)} %get-tuple-element.9) | data formatting | bytes 8388608 | tf_op jit(solution)/shard_map/reshape | solution.py:172
  502.4 9.0 %copy.49 = bf16[256,32,2,128]{0,1,2,3:T(8,128)(2,1)} copy(bf16[256,32,2,128]{3,2,1,0:T(2,128)(2,1)} %reshape.147) | data formatting | bytes 8388608 | tf_op jit(solution)/shard_map/reshape | solution.py:172
  511.4 9.0 %subtract_convert_fusion = (bf16[8,16,256,128]{3,2,1,0:T(8,128)(2,1)}, bf16[8,16,256,128]{3,2,1,0:T(8,128)(2,1)}) fusion(f32[16,256,128]{2,1,0:T(8,128)} %get-tuple-element.21, f32[8,256,128]{2,1,0:T(8,128)} %get-tuple-element.19, f32[16,256,128]{2,1,0:T(8,128)S(1)} %get-tuple-element.20, f32[8,256,128]{2,1,0:T(8,128)S(1)} %get-tuple-element.18), kind=kLoop, calls=%fused_computation.11 | loop fusion | flops 33554432 | bytes 23068672 | tf_op jit(solution)/shard_map/convert_element_type | solution.py:164
  520.4 12.6 %fusion.4 = f32[128,64,256]{2,1,0:T(8,128)} fusion(bf16[128,64,256]{2,1,0:T(8,128)(2,1)} %bitcast.56, bf16[128,256,128]{2,1,0:T(8,128)(2,1)} %bitcast.54, bf16[128,256,128]{2,1,0:T(8,128)(2,1)} %bitcast.52), kind=kOutput, calls=%fused_computation.12 | convolution fusion | flops 1107296256 | bytes 29360128 | tf_op jit(solution)/shard_map/frk,fkd->frd/dot_general | solution.py:174
  533.0 4.6 fusion.10
  538.0 6.9 %reshape.144 = bf16[256,32,2,128]{3,2,1,0:T(2,128)(2,1)} reshape(bf16[256,32,256]{2,1,0:T(8,128)(2,1)} %get-tuple-element.10) | data formatting | bytes 8388608 | tf_op jit(solution)/shard_map/reshape | solution.py:172
  544.9 9.0 %copy.44 = bf16[256,32,2,128]{0,1,2,3:T(8,128)(2,1)} copy(bf16[256,32,2,128]{3,2,1,0:T(2,128)(2,1)} %reshape.144) | data formatting | bytes 8388608 | tf_op jit(solution)/shard_map/reshape | solution.py:172
  553.9 12.6 %fusion.5 = f32[128,64,256]{2,1,0:T(8,128)} fusion(bf16[128,64,256]{2,1,0:T(8,128)(2,1)} %bitcast.57, bf16[128,256,128]{2,1,0:T(8,128)(2,1)} %bitcast.55, bf16[128,256,128]{2,1,0:T(8,128)(2,1)} %bitcast.53), kind=kOutput, calls=%fused_computation.13 | convolution fusion | flops 1107296256 | bytes 29360128 | tf_op jit(solution)/shard_map/frk,fkd->frd/dot_general | solution.py:174
  566.5 4.6 slice_subtract_fusion.1
  571.5 52.4 %collective-permute-done = bf16[128,32,256]{2,1,0:T(8,128)(2,1)} collective-permute-done((bf16[128,32,256]{2,1,0:T(8,128)(2,1)S(1)}, bf16[128,32,256]{2,1,0:T(8,128)(2,1)}, u32[]{:S(2)}, u32[]{:S(2)}) %collective-permute-start) | collective-permute-done | bytes 2097184 | tf_op jit(solution)/shard_map/ppermute | solution.py:219
  623.9 3.8 add_convert_fusion.1
  627.7 3.5 copy.54
  631.2 2.7 bitcast_multiply_fusion
  (23 shorter events, 9.3 us)
Async XLA Ops:
  13.1 26.4 %copy-start.1 = (s32[512,512]{1,0:T(8,128)S(1)}, s32[512,512]{1,0:T(8,128)}, u32[]{:S(2)}) copy-start(s32[512,512]{1,0:T(8,128)} %param.8) | copy-start | bytes 3145732
  54.9 5.5 copy-start
  474.8 6.1 copy-start.2
  537.9 86.0 %collective-permute-start = (bf16[128,32,256]{2,1,0:T(8,128)(2,1)S(1)}, bf16[128,32,256]{2,1,0:T(8,128)(2,1)}, u32[]{:S(2)}, u32[]{:S(2)}) collective-permute-start(bf16[128,32,256]{2,1,0:T(8,128)(2,1)S(1)} %pad_maximum_fusion.5), channel_id=1, source_target_pairs={{0,8},{1,9},{2,10},{3,11},{4,12},{5,13},{6,14},{7,15},{8,0},{9,1},... | collective-permute-start | bytes 6291464 | tf_op jit(solution)/shard_map/ppermute | solution.py:219
  627.7 3.5 copy-start.3
